TPU v7x, 32 devices: a whole 2x2x4 slice. The times are simulated.
32 devices in a mesh: section: 2 (over y), dp: 16 (over z, x, core).
Axes of the slice: x: 2, y: 2, z: 4, core: 2. Of those that a mesh axis runs over, the one named last changes fastest.
Arguments:
- frames: bfloat16 [2, 32, 42, 64, 192], P('section', 'dp'), may hold values from -4 to 4
- action_ids: int32 [2, 32, 42], P('section', 'dp'), may hold values from 0 to 16
- delta_ids: int32 [2, 32, 42, 4], P('section', 'dp'), may hold values from 0 to 1023
- seq_len: int32 [2, 32], P(None, 'dp'), may hold values from 8 to 21, as said below
- enc_w1: bfloat16 [48, 128], replicated, may hold values from -0.875 to 0.875
- enc_w2: bfloat16 [512, 512], replicated, may hold values from -0.25 to 0.25
- codebook: bfloat16 [1024, 512], replicated, may hold values from -6 to 6
- action_table: bfloat16 [17, 512], replicated, may hold values from -6 to 6
- ln_gain: float32 [2, 512, 2], replicated, may hold values from 0.25 to 1.75
- ln_bias: float32 [2, 512, 2], replicated, may hold values from -2 to 2
- w_qkv: bfloat16 [2, 512, 1536], replicated, may hold values from -0.25 to 0.25
- w_out: bfloat16 [2, 512, 512], replicated, may hold values from -1 to 1
- w_up: bfloat16 [2, 512, 2048], replicated, may hold values from -0.25 to 0.25
- w_down: bfloat16 [2, 2048, 512], replicated, may hold values from -0.125 to 0.125
- cotangent: bfloat16 [2, 32, 252, 512], P('section', 'dp'), may hold values from -6 to 6
Outputs:
- activations: bfloat16 [2, 32, 252, 512], P('section', 'dp')
- embed_grad: bfloat16 [2, 32, 252, 512], P('section', 'dp')
- grad_qkv: float32 [2, 2, 512, 1536], P('section', None, 'dp')
- grad_out: float32 [2, 2, 512, 512], P('section', None, 'dp')
- grad_up: float32 [2, 2, 512, 2048], P('section', None, 'dp')
- grad_down: float32 [2, 2, 2048, 512], P('section', None, 'dp')
- grad_gain: float32 [2, 2, 512, 2], P('section', None, 'dp')
- grad_bias: float32 [2, 2, 512], P('section', None, 'dp')
- grad_bias_two: float32 [2, 2, 512], P('section', None, 'dp')
- grad_enc1: float32 [2, 48, 128], P('section', None, 'dp')
- grad_enc2: float32 [2, 512, 512], P('section', None, 'dp')
- grad_codebook: float32 [2, 1024, 512], P('section', None, 'dp')
- grad_actions: float32 [2, 17, 512], P('section', None, 'dp')
Inputs may be any that keep to these rules, and one draw needn't show every extreme that they name: `seq_len`: each entry is 8 or 21; the 42 steps of a micro-batch form sequences of that many steps one after the other, the last one shorter where it does not divide 42; both values occur in every draw.
All inputs are finite; a program needn't handle non-finite values.
Results may differ from a plain program's by a relative error of at most 0.019.
Values may be sent and summed in bfloat16 or wider, within the bound.
A program may use at most 256 MiB of HBM per device.

v0:
```python
import functools

import jax
import jax.numpy as jnp
from jax import lax
from jax.experimental import pallas as pl
from jax.experimental.pallas import tpu as pltpu
from jax.sharding import PartitionSpec as P

HEADS = 8
HEAD_DIM = 64
TPS = 6
EPS = 1e-05
BF = jnp.bfloat16
F32 = jnp.float32
I32 = jnp.int32

WIDTH = 512
CODES = 1024
FRAMES_BLOCK = 28
BLOCK_ROWS = FRAMES_BLOCK * 8
TABLE = 1152
POOL_AT = 1056
ACT_AT = 1024
LAYER_COLS = 6144
ENC_COLS = 1664
VMEM_LIMIT = 60 << 20
TRAIN_VMEM = 63 << 20
PLAN = "00000000010111000000001111110101010101012"


def dot(a, b):
    return jnp.dot(a, b, preferred_element_type=F32)


def dot_rows(a, b):
    return lax.dot_general(a, b, (((0,), (0,)), ((), ())), preferred_element_type=F32)


def dot_lanes(a, b):
    return lax.dot_general(a, b, (((1,), (1,)), ((), ())), preferred_element_type=F32)


def iota(shape, axis):
    return lax.broadcasted_iota(I32, shape, axis)


def gelu_pair(v):
    cdf = 0.5 + 0.5 * lax.erf(v * 0.7071067811865476)
    bell = jnp.exp2(v * v * (-0.5 * 1.4426950408889634))
    return v * cdf, cdf + v * (bell * 0.3989422804014327)


def gelu(v):
    return v * (0.5 + 0.5 * lax.erf(v * 0.7071067811865476))


def gelu_slope(v):
    return gelu_pair(v.astype(F32))[1]


def patch_index(rows):
    k = iota((rows, 48), 0)
    dy = (k * 2731) >> 16
    rest = k - dy * 24
    j = jnp.where(rest >= 12, rest - 12, rest)
    return jnp.where((iota((rows, 48), 1) == dy * 12 + j) & (k < 96), 1.0, 0.0), rest


def encoder_weights(w1):
    hot, rest = patch_index(128)
    wide = dot(hot.astype(BF), w1)
    first = jnp.where(rest[:, :1] < 12, wide, 0.0)
    second = jnp.where(rest[:, :1] >= 12, wide, 0.0)
    block = jnp.concatenate([first, second], axis=1)
    zero = jnp.zeros_like(block)
    return jnp.concatenate(
        [jnp.concatenate([block, zero], axis=1), jnp.concatenate([zero, block], axis=1)], axis=0
    ).astype(BF)


def token_ids(s, names, deltas):
    steps = names.shape[1]
    frame = s * steps + iota((1, steps), 1)
    block = (frame * 2341) >> 16
    pool = POOL_AT + block * 32 + frame - FRAMES_BLOCK * block
    kinds = jnp.concatenate([pool, names[s : s + 1] + ACT_AT, deltas[s]], axis=0).astype(F32)
    row = iota((256, 1), 0)
    step = (row * 10923) >> 16
    hot = jnp.where(iota((256, steps), 1) == step, 1.0, 0.0)
    each = lax.dot_general(
        hot, kinds, (((1,), (1,)), ((), ())), preferred_element_type=F32,
        precision=lax.Precision.HIGHEST,
    )
    mine = jnp.where(iota((256, TPS), 1) == row - TPS * step, each, 0.0)
    found = (jnp.sum(mine, axis=1, keepdims=True) + 0.5).astype(I32)
    return jnp.where(row < TPS * steps, found, -1)


def enc_fwd_kernel(
    frames, w1, w2, book, acts, names, deltas,
    tok, ids, xl, blocks, z1, z2, perm, lanes, big, xs, acc, table,
):
    step = pl.program_id(0)

    @pl.when(step == 0)
    def _():
        a, b = iota((256, 256), 0), iota((256, 256), 1)
        perm[...] = jnp.where(b == 8 * (a & 31) + (a >> 5), 1.0, 0.0).astype(BF)
        src = iota((256, 1024), 0)
        px = (src * 5462) >> 16
        at = (px >> 1) * 128 + (px & 1) * 12 + (src - px * 12)
        out = jnp.where(src < 192, iota((256, 1024), 1) - at, -1)
        for dy in range(4):
            lanes[pl.ds(256 * dy, 256), :] = jnp.where(out == dy * 24, 1.0, 0.0).astype(BF)
        xs[...] = jnp.zeros_like(xs)
        big[...] = encoder_weights(w1[...])
        table[pl.ds(0, CODES), :] = book[...]
        named = acts[...].astype(F32)
        pad = jnp.zeros((TABLE - ACT_AT - named.shape[0], WIDTH), F32)
        table[pl.ds(ACT_AT, TABLE - ACT_AT), :] = jnp.concatenate([named, pad], axis=0).astype(BF)

    for group in range(FRAMES_BLOCK // 4):
        rows = frames[pl.ds(group * 4, 4)].reshape(256, 192)
        moved = dot(perm[...], rows).astype(BF).reshape(2, 4, 32, 192)
        for dy in range(4):
            xs[:, pl.ds(group * 32, 32), pl.ds(256 * dy, 192)] = moved[:, dy]
    for dy2 in range(2):
        spread = dot(xs[dy2], lanes[...]).astype(BF)
        for bx in range(8):
            xl[0, pl.ds(bx * BLOCK_ROWS, BLOCK_ROWS), pl.ds(dy2 * 128, 128)] = spread[
                :, bx * 128 : (bx + 1) * 128
            ]
    acc[...] = jnp.zeros_like(acc)

    def part(bx, _):
        rows = pl.ds(pl.multiple_of(bx * BLOCK_ROWS, BLOCK_ROWS), BLOCK_ROWS)
        first = dot(xl[0, rows, :], big[...])
        z1[0, rows, :] = first.astype(BF)
        value = gelu(first).astype(BF)
        blocks[0, rows, :] = value
        second = dot(value, w2[...])
        z2[0, rows, :] = second.astype(BF)
        acc[...] += gelu(second)
        return 0

    lax.fori_loop(0, 8, part, 0, unroll=True)
    pooled = jnp.sum(acc[...].reshape(FRAMES_BLOCK, 8, WIDTH), axis=1) * (1.0 / 64.0)
    pooled = jnp.concatenate([pooled, jnp.zeros((32 - FRAMES_BLOCK, WIDTH), F32)], axis=0)
    table[pl.ds(pl.multiple_of(POOL_AT + step * 32, 32), 32), :] = pooled.astype(BF)

    @pl.when(step == pl.num_programs(0) - 1)
    def _():
        for s in range(2):
            rows = pl.ds(s * 256, 256)
            found = token_ids(s, names[...], deltas[...])
            ids[rows, :] = found
            hot = jnp.where(iota((256, TABLE), 1) == found, 1.0, 0.0).astype(BF)
            tok[rows, :] = dot(hot, table[...]).astype(BF)


def enc_forward(frames, w1, w2, book, acts, names, deltas):
    count = frames.shape[0]
    grid = count // FRAMES_BLOCK
    rows = 8 * BLOCK_ROWS

    def whole(shape):
        return pl.BlockSpec(shape, lambda i: (0,) * len(shape))

    def saved(lanes):
        return pl.BlockSpec((1, rows, lanes), lambda i: (i, 0, 0))

    return pl.pallas_call(
        enc_fwd_kernel,
        grid=(grid,),
        in_specs=[
            pl.BlockSpec((FRAMES_BLOCK, 64, 192), lambda i: (i, 0, 0)),
            whole(w1.shape),
            whole(w2.shape),
            whole(book.shape),
            whole(acts.shape),
            whole(names.shape),
            whole(deltas.shape),
        ],
        out_specs=[
            whole((512, WIDTH)), whole((512, 1)), saved(256), saved(512), saved(512), saved(512),
        ],
        out_shape=[
            jax.ShapeDtypeStruct((512, WIDTH), BF),
            jax.ShapeDtypeStruct((512, 1), I32),
            jax.ShapeDtypeStruct((grid, rows, 256), BF),
            jax.ShapeDtypeStruct((grid, rows, 512), BF),
            jax.ShapeDtypeStruct((grid, rows, 512), BF),
            jax.ShapeDtypeStruct((grid, rows, 512), BF),
        ],
        scratch_shapes=[
            pltpu.VMEM((256, 256), BF),
            pltpu.VMEM((1024, 1024), BF),
            pltpu.VMEM((256, 512), BF),
            pltpu.VMEM((2, BLOCK_ROWS, 1024), BF),
            pltpu.VMEM((BLOCK_ROWS, WIDTH), F32),
            pltpu.VMEM((TABLE, WIDTH), BF),
        ],
        compiler_params=pltpu.CompilerParams(vmem_limit_bytes=VMEM_LIMIT),
        name="enc_fwd",
    )(frames, w1, w2, book, acts, names, deltas)


def ln_parts(x):
    mean = jnp.mean(x, axis=-1, keepdims=True)
    center = x - mean
    var = jnp.mean(center * center, axis=-1, keepdims=True)
    scale = lax.rsqrt(var + EPS)
    return center * scale, scale


def ln_back(x, d, gain):
    hat, scale = ln_parts(x)
    dh = d * gain
    one = jnp.mean(dh, axis=-1, keepdims=True)
    two = jnp.mean(dh * hat, axis=-1, keepdims=True)
    back = scale * (dh - one - hat * two)
    return back, jnp.sum(d * hat, axis=0, keepdims=True), jnp.sum(d, axis=0, keepdims=True)


def head_mask(h):
    lane = iota((1, 256), 1) >> 6
    return lane == h


def stacked(rows, scale):
    out = []
    for h in range(4):
        mask = jnp.where(head_mask(h), scale, 0.0).astype(BF)
        out.append(rows * mask)
    return jnp.concatenate(out, axis=0)


def unstacked(rows):
    out = rows[768:]
    for h in range(3):
        out = jnp.where(head_mask(h), rows[h * 256 : (h + 1) * 256], out)
    return out


def scatter_rows(g, d, cols, value, dests=16):
    shaped = value.astype(BF).reshape(dests // 2, 2, 32, value.shape[1])
    for core in range(2):
        g[d, core, :, :, cols] = shaped[:, core]


def layers_kernel(
    tok, cot_h, lens, lnp, wq_h, wo_h, wu_h, wd_h,
    act, eg, g, gl,
    wq, wo, wu, wd, stream, normed, packed, probs, att, normed2, gated, slope, bias,
    up, back_up, back_att, back_packed, lng, cot, mine, theirs, sems, cross_sem,
):
    layers = wq.shape[0]
    section = lax.axis_index("section")
    barrier = pltpu.get_barrier_semaphore()
    pl.semaphore_signal(
        barrier, inc=1, device_id=(1 - section, lax.axis_index("dp")), device_id_type=MESH
    )
    pl.semaphore_wait(barrier, 1)
    cot_copy = cross_copy(cot_h, cot, cross_sem.at[0])
    cot_copy.start()
    act_copy = cross_copy(mine, theirs, cross_sem.at[1])
    copies = []
    for d in range(layers):
        for k, (src, dst) in enumerate(((wq_h, wq), (wo_h, wo), (wu_h, wu), (wd_h, wd))):
            copy = pltpu.make_async_copy(src.at[d], dst.at[d], sems.at[d, k])
            copy.start()
            copies.append(copy)

    stream[0, 0] = tok[...].astype(F32)
    row = iota((256, 1), 0)
    col = iota((1, 256), 1)
    q_step = ((row * 10923) >> 16).astype(F32)
    k_step = ((col * 10923) >> 16).astype(F32)
    for s in range(2):
        inv = 1.0 / lens[section, s].astype(F32)
        q_seq = jnp.floor((q_step + 0.5) * inv)
        k_seq = jnp.floor((k_step + 0.5) * inv)
        bias[s] = jnp.where((k_step <= q_step) & (q_seq == k_seq), 0.0, -1e30)
    for copy in copies:
        copy.wait()

    def forward(d, _):
        x = stream[d, 0]
        hat, _ = ln_parts(x)
        normed[d] = (hat * lnp[d, 0:1] + lnp[d, 2:3]).astype(BF)
        for c in range(3):
            cols = pl.ds(c * 512, 512)
            packed[d, :, cols] = dot(normed[d], wq[d, :, cols]).astype(BF)
        for s in range(2):
            rows = pl.ds(s * 256, 256)
            for quad in range(2):
                q = stacked(packed[d, rows, pl.ds(quad * 256, 256)], HEAD_DIM**-0.5)
                k = packed[d, rows, pl.ds(512 + quad * 256, 256)]
                v = packed[d, rows, pl.ds(1024 + quad * 256, 256)]
                scores = dot_lanes(q, k).reshape(4, 256, 256) + bias[s][None]
                top = jnp.max(scores, axis=-1, keepdims=True)
                e = jnp.exp(scores - top)
                total = jnp.sum(e, axis=-1, keepdims=True)
                p = (e * (1.0 / total)).astype(BF).reshape(1024, 256)
                probs[d, s * 2 + quad] = p
                att[d, rows, pl.ds(quad * 256, 256)] = unstacked(dot(p, v)).astype(BF)
        middle = stream[d, 0] + dot(att[d], wo[d])
        stream[d, 1] = middle
        hat, _ = ln_parts(middle)
        normed2[d] = (hat * lnp[d, 1:2] + lnp[d, 3:4]).astype(BF)

        def chunk(c, _):
            cols = pl.ds(pl.multiple_of(c * 512, 512), 512)
            value, grad = gelu_pair(dot(normed2[d], wu[d, :, cols]))
            gated[d, :, cols] = value.astype(BF)
            slope[d, :, cols] = grad.astype(BF)
            return 0

        lax.fori_loop(0, 4, chunk, 0)
        stream[d + 1, 0] = stream[d, 1] + dot(gated[d], wd[d])
        return 0

    lax.fori_loop(0, layers, forward, 0)
    cot_copy.wait()
    mine[...] = stream[layers, 0].astype(BF)
    act_copy.start()
    for s in range(2):
        up[pl.ds(s * 256, 252), :] = cot[s].astype(F32)
        up[pl.ds(s * 256 + 252, 4), :] = jnp.zeros((4, WIDTH), F32)
    lng[...] = jnp.zeros_like(lng)

    def backward(i, _):
        d = layers - 1 - i
        down = up[...].astype(BF)

        def chunk(c, _):
            cols = pl.ds(pl.multiple_of(c * 256, 256), 256)
            part = dot_rows(gated[d, :, cols], down).astype(BF).reshape(2, 4, 32, WIDTH)
            for core in range(2):
                for j in range(4):
                    g[d, core, c, :, pl.ds(4096 + 512 * j, 512)] = part[core, j]
            back = dot_lanes(down, wd[d, cols, :])
            back = (back * slope[d, :, cols].astype(F32)).astype(BF)
            back_up[:, cols] = back
            part = dot_rows(normed2[d], back).astype(BF).reshape(8, 2, 32, 256)
            out = pl.ds(pl.multiple_of(2048 + c * 256, 256), 256)
            for core in range(2):
                g[d, core, :, :, out] = part[:, core]
            return 0

        lax.fori_loop(0, 8, chunk, 0)
        back, gain, shift = ln_back(stream[d, 1], dot_lanes(back_up[...], wu[d]), lnp[d, 1:2])
        lng[pl.ds(d * 4 + 1, 1), :] = gain
        lng[pl.ds(d * 4 + 3, 1), :] = shift
        up[...] += back
        branch = up[...].astype(BF)
        scatter_rows(g, d, pl.ds(1536, 512), dot_rows(att[d], branch))
        back_att[...] = dot_lanes(branch, wo[d]).astype(BF)
        for s in range(2):
            rows = pl.ds(s * 256, 256)
            for quad in range(2):
                lanes = pl.ds(quad * 256, 256)
                qs = stacked(packed[d, rows, lanes], HEAD_DIM**-0.5)
                k = packed[d, rows, pl.ds(512 + quad * 256, 256)]
                v = packed[d, rows, pl.ds(1024 + quad * 256, 256)]
                outs = stacked(back_att[rows, lanes], 1.0)
                p = probs[d, s * 2 + quad]
                dp = dot_lanes(outs, v)
                pf = p.astype(F32)
                weighted = pf * dp
                total = jnp.sum(weighted, axis=-1, keepdims=True)
                ds = (weighted - pf * total).astype(BF)
                back_packed[rows, lanes] = (unstacked(dot(ds, k)) * HEAD_DIM**-0.5).astype(BF)
                back_packed[rows, pl.ds(512 + quad * 256, 256)] = dot_rows(ds, qs).astype(BF)
                back_packed[rows, pl.ds(1024 + quad * 256, 256)] = dot_rows(p, outs).astype(BF)
        for c in range(3):
            cols = pl.ds(c * 512, 512)
            scatter_rows(g, d, cols, dot_rows(normed[d], back_packed[:, cols]))
        back, gain, shift = ln_back(stream[d, 0], dot_lanes(back_packed[...], wq[d]), lnp[d, 0:1])
        lng[pl.ds(d * 4, 1), :] = gain
        lng[pl.ds(d * 4 + 2, 1), :] = shift
        up[...] += back
        return 0

    lax.fori_loop(0, layers, backward, 0)
    eg[...] = up[...].astype(BF)
    act_copy.wait()
    for s in range(2):
        act[s] = theirs[pl.ds(s * 256, 256), :].astype(F32)[:252].astype(BF)
    turned = jnp.transpose(lng[...]).astype(BF).reshape(8, 2, 32, 128)
    for core in range(2):
        gl[core] = turned[:, core]


def run_layers(tok, cot, lens, lnp, wq, wo, wu, wd):
    layers = wq.shape[0]
    vm = pl.BlockSpec(memory_space=pltpu.VMEM)
    sm = pl.BlockSpec(memory_space=pltpu.SMEM)
    hb = pl.BlockSpec(memory_space=pl.ANY)
    rows = 512
    return pl.pallas_call(
        layers_kernel,
        in_specs=[vm, hb, sm, vm, hb, hb, hb, hb],
        out_specs=[vm, vm, vm, vm],
        out_shape=[
            jax.ShapeDtypeStruct((2, 252, WIDTH), BF),
            jax.ShapeDtypeStruct((rows, WIDTH), BF),
            jax.ShapeDtypeStruct((layers, 2, 8, 32, LAYER_COLS), BF),
            jax.ShapeDtypeStruct((2, 8, 32, 128), BF),
        ],
        scratch_shapes=[
            pltpu.VMEM(wq.shape, BF),
            pltpu.VMEM(wo.shape, BF),
            pltpu.VMEM(wu.shape, BF),
            pltpu.VMEM(wd.shape, BF),
            pltpu.VMEM((layers + 1, 2, rows, WIDTH), F32),
            pltpu.VMEM((layers, rows, WIDTH), BF),
            pltpu.VMEM((layers, rows, 3 * WIDTH), BF),
            pltpu.VMEM((layers, 4, 1024, 256), BF),
            pltpu.VMEM((layers, rows, WIDTH), BF),
            pltpu.VMEM((layers, rows, WIDTH), BF),
            pltpu.VMEM((layers, rows, 4 * WIDTH), BF),
            pltpu.VMEM((layers, rows, 4 * WIDTH), BF),
            pltpu.VMEM((2, 256, 256), F32),
            pltpu.VMEM((rows, WIDTH), F32),
            pltpu.VMEM((rows, 4 * WIDTH), BF),
            pltpu.VMEM((rows, WIDTH), BF),
            pltpu.VMEM((rows, 3 * WIDTH), BF),
            pltpu.VMEM((128, WIDTH), F32),
            pltpu.VMEM(cot.shape, BF),
            pltpu.VMEM((rows, WIDTH), BF),
            pltpu.VMEM((rows, WIDTH), BF),
            pltpu.SemaphoreType.DMA((layers, 4)),
            pltpu.SemaphoreType.DMA((2, 2)),
        ],
        compiler_params=pltpu.CompilerParams(
            collective_id=1, has_side_effects=True, vmem_limit_bytes=VMEM_LIMIT
        ),
        name="layers",
    )(tok, cot, lens, lnp, wq, wo, wu, wd)


def enc_bwd_kernel(eg, xl, blocks, g1, g2, w2, ids, e, dpool, bs, bf, acc2, acc1):
    step = pl.program_id(0)

    @pl.when(step == 0)
    def _():
        hot = jnp.where(iota((512, TABLE), 1) == ids[...], 1.0, 0.0).astype(BF)
        code = dot_rows(eg[...], hot[:, :POOL_AT + 96]).astype(BF)
        dpool[...] = dot_rows(hot[:, POOL_AT : POOL_AT + 96], eg[...])
        parts = code[:, :CODES].reshape(8, 2, 32, CODES)
        tail = code[:, CODES : CODES + 128].reshape(8, 2, 32, 128)
        for core in range(2):
            e[core, :, :, pl.ds(512, CODES)] = parts[:, core]
            e[core, :, :, pl.ds(1536, 128)] = tail[:, core]
        acc2[...] = jnp.zeros_like(acc2)
        acc1[...] = jnp.zeros_like(acc1)

    pooled = dpool[pl.ds(pl.multiple_of(step * 32, 32), 32), :][:FRAMES_BLOCK] * (1.0 / 64.0)
    wide = jnp.broadcast_to(pooled[:, None, :], (FRAMES_BLOCK, 8, WIDTH)).reshape(BLOCK_ROWS, WIDTH)

    def part(bx, _):
        rows = pl.ds(pl.multiple_of(bx * BLOCK_ROWS, BLOCK_ROWS), BLOCK_ROWS)
        back = (wide * gelu_slope(g2[0, rows, :])).astype(BF)
        bs[rows, :] = back
        bf[rows, :] = (dot_lanes(back, w2[...]) * gelu_slope(g1[0, rows, :])).astype(BF)
        return 0

    lax.fori_loop(0, 8, part, 0)
    acc2[...] += dot_rows(bs[...], blocks[0])
    for dy2 in range(2):
        acc1[:, pl.ds(dy2 * 256, 256)] += dot_rows(
            xl[0, :, pl.ds(dy2 * 128, 128)], bf[:, pl.ds(dy2 * 256, 256)]
        )

    @pl.when(step == pl.num_programs(0) - 1)
    def _():
        parts = acc2[...].astype(BF).reshape(8, 2, 32, WIDTH)
        both = acc1[:, pl.ds(0, 256)] + acc1[:, pl.ds(256, 256)]
        hot, rest = patch_index(128)
        first = jnp.where(rest[:, :1] < 12, both[:, :128], both[:, 128:])
        first = lax.dot_general(
            first, hot, (((0,), (0,)), ((), ())), preferred_element_type=F32,
            precision=lax.Precision.HIGHEST,
        )
        first = first.reshape(8, 2, 8, 48)
        first = jnp.concatenate([first, jnp.zeros((8, 2, 24, 48), F32)], axis=2).astype(BF)
        for core in range(2):
            e[core, :, :, pl.ds(0, WIDTH)] = parts[:, core]
            e[core, :, :, pl.ds(1536 + 64, 48)] = first[:, core]


def enc_backward(eg, xl, blocks, g1, g2, w2, ids):
    grid, rows, _ = xl.shape

    def whole(shape):
        return pl.BlockSpec(shape, lambda i: (0,) * len(shape))

    def saved(lanes):
        return pl.BlockSpec((1, rows, lanes), lambda i: (i, 0, 0))

    return pl.pallas_call(
        enc_bwd_kernel,
        grid=(grid,),
        in_specs=[
            whole(eg.shape), saved(256), saved(512), saved(512), saved(512),
            whole(w2.shape), whole(ids.shape),
        ],
        out_specs=whole((2, 8, 32, ENC_COLS)),
        out_shape=jax.ShapeDtypeStruct((2, 8, 32, ENC_COLS), BF),
        scratch_shapes=[
            pltpu.VMEM((96, WIDTH), F32),
            pltpu.VMEM((rows, WIDTH), BF),
            pltpu.VMEM((rows, WIDTH), BF),
            pltpu.VMEM((WIDTH, WIDTH), F32),
            pltpu.VMEM((128, WIDTH), F32),
        ],
        compiler_params=pltpu.CompilerParams(vmem_limit_bytes=VMEM_LIMIT),
        name="enc_bwd",
    )(eg, xl, blocks, g1, g2, w2, ids)


CHIPS = 8
HOPS = CHIPS // 2
MESH = pl.DeviceIdType.MESH


def ring_place(chip):
    z, x = chip // 2, chip % 2
    return z * (1 - x) + (7 - z) * x


def ring_chip(place):
    half = place // 4
    return (1 - half) * (2 * place) + half * (15 - 2 * place)


def where_am_i():
    section, me = lax.axis_index("section"), lax.axis_index("dp")
    core, chip = me % 2, me // 2
    place = ring_place(chip)
    ahead = ring_chip((place + 1) % CHIPS) * 2 + core
    behind = ring_chip((place + CHIPS - 1) % CHIPS) * 2 + core
    sibling = chip * 2 + (1 - core)
    return section, me, core, place, ahead, behind, sibling


def greet():
    section, me, _, _, ahead, behind, sibling = where_am_i()
    barrier = pltpu.get_barrier_semaphore()
    for target in ((section, sibling), (section, ahead), (section, behind), (1 - section, me)):
        pl.semaphore_signal(barrier, inc=1, device_id=target, device_id_type=MESH)
    pl.semaphore_wait(barrier, 4)


def cross_copy(src, dst, sem):
    section, me = lax.axis_index("section"), lax.axis_index("dp")
    return pltpu.make_async_remote_copy(
        src_ref=src, dst_ref=dst, send_sem=sem.at[0], recv_sem=sem.at[1],
        device_id=(1 - section, me), device_id_type=MESH,
    )


def turn(rows):
    tall = jnp.concatenate([rows, jnp.zeros((96, rows.shape[1]), F32)], axis=0)
    return jnp.transpose(tall)[:, :32]


ACT_NORMED, ACT_Q, ACT_PROBS, ACT_ATT, ACT_NORMED2, ACT_GATED, ACT_SLOPE = 0, 1, 4, 8, 9, 10, 14
ACT_PANELS = 18
W_QKV, W_OUT, W_UP, W_DOWN = 0, 3, 4, 8
W_PANELS = 12


def panel(ref, d, p):
    return ref[d, pl.ds(2 * p, 2)].reshape(512, WIDTH)


def put_panel(ref, d, p, value):
    ref[d, pl.ds(2 * p, 2)] = value.astype(BF).reshape(2, 8, 32, WIDTH)


def quarter(ref, d, p, s, quad):
    return ref[d, 2 * p + s, :, :, pl.ds(256 * quad, 256)].reshape(256, 256)


def put_quarter(ref, d, p, s, quad, value):
    ref[d, 2 * p + s, :, :, pl.ds(256 * quad, 256)] = value.astype(BF).reshape(8, 32, 256)


def side_by_side(ref, d, p, count):
    return jnp.concatenate([panel(ref, d, p + c) for c in range(count)], axis=1)


class Piece:
    def __init__(self, own, pair, hop, mine, sems):
        self.own, self.pair, self.hop, self.mine = own, pair, hop, mine
        self.pair_sem, self.send_sem, self.recv_sem = sems

    def pair_copy(self):
        section, _, core, _, _, _, sibling = where_am_i()
        return pltpu.make_async_remote_copy(
            src_ref=self.own(1 - core), dst_ref=self.pair,
            send_sem=self.pair_sem.at[0], recv_sem=self.pair_sem.at[1],
            device_id=(section, sibling), device_id_type=MESH,
        )

    def target(self, way, step):
        place, far = where_am_i()[3], HOPS - step
        return ring_chip((place + (far if way == 0 else CHIPS - far)) % CHIPS)

    def rows(self, way, step):
        return pl.ds(0, 32) if step else pl.ds(16 * way, 16)

    def hop_copy(self, way, step):
        section, _, _, _, ahead, behind, _ = where_am_i()
        return pltpu.make_async_remote_copy(
            src_ref=self.pair.at[:, self.target(way, step), self.rows(way, step), :],
            dst_ref=self.hop(way, step),
            send_sem=self.send_sem.at[way, step], recv_sem=self.recv_sem.at[way, step],
            device_id=(section, ahead if way == 0 else behind), device_id_type=MESH,
        )

    def both(self, n, at, rows):
        core = where_am_i()[2]
        return self.own(core)[n, at, rows, :].astype(F32) + self.pair[n, at, rows, :].astype(F32)

    def each(self, body):
        def run(n, _):
            body(n)
            return 0

        lax.fori_loop(0, self.pair.shape[0], run, 0)

    def send(self, step):
        for way in range(2):
            if step:
                self.hop_copy(way, step - 1).wait()
            at = self.target(way, step)

            def add(n):
                for half in range(2):
                    if step == 0 and half != way:
                        continue
                    rows = pl.ds(16 * half, 16)
                    value = self.both(n, at, rows)
                    if step == 1 and half == way:
                        value += self.hop(way, 0)[n].astype(F32)
                    elif step > 1:
                        value += self.hop(way, step - 1)[n, rows, :].astype(F32)
                    self.pair[n, at, rows, :] = value.astype(BF)

            self.each(add)
            self.hop_copy(way, step).start()

    def close(self):
        at = ring_chip(where_am_i()[3])
        for way in range(2):
            self.hop_copy(way, HOPS - 1).wait()

        def add(n):
            value = self.both(n, at, pl.ds(0, 32))
            for way in range(2):
                value += self.hop(way, HOPS - 1)[n].astype(F32)
            self.mine[n] = value.astype(self.mine.dtype)

        self.each(add)


class Stream:
    def __init__(self, pieces, crossings):
        self.pieces, self.crossings = pieces, crossings

    def pair(self):
        for piece in self.pieces:
            piece.pair_copy().start()

    def open(self):
        for piece in self.pieces:
            piece.pair_copy().wait()
            piece.send(0)

    def send(self, step):
        for piece in self.pieces:
            piece.send(step)

    def close(self):
        for piece in self.pieces:
            piece.close()
        for crossing in self.crossings:
            cross_copy(*crossing).start()


class Traffic:
    def __init__(self, plan):
        self.queue, self.plan = [], plan

    def add(self, stream):
        self.queue.append((stream, 1))

    def take(self, count=None):
        if count is None:
            count, self.plan = int(self.plan[0]), self.plan[1:]
        hops = []
        while count and self.queue:
            stream, step = self.queue.pop(0)
            hops.append((stream, step))
            if step < HOPS:
                self.queue.append((stream, step + 1))
            count -= 1
        return hops


def issue(hops):
    for stream, step in hops:
        if step < HOPS:
            stream.send(step)
        else:
            stream.close()


def train_kernel(
    tok, cot_h, lens, gains, shifts, wq_h, wo_h, wu_h, wd_h, xl_h, bl_h, z1_h, z2_h, w2, ids,
    act, eg, late, early, norm, enc, misc,
    wts, acts, hop1, xin, mid, bias, back_att, lng, cot, act_mine, act_theirs,
    mine1, theirs1, mine0, theirs0, lnown, lnpair, lnhop, lnmine, lntheirs,
    genc, enc_mine, miscown, miscpair, mischop, miscmine, acc2, acc1, dpool,
    load_sem, stream_sem, cross_sem, pair_sem, send_sem, recv_sem, free_sem,
):
    section, me, core, _, ahead, behind, sibling = where_am_i()
    greet()
    cot_copy = cross_copy(cot_h, cot, cross_sem.at[0])
    cot_copy.start()
    act_copy = cross_copy(act_mine, act_theirs, cross_sem.at[1])
    for d in range(2):
        for c in range(W_PANELS):
            if c < 3:
                src = wq_h.at[d, :, :, :, pl.ds(512 * c, 512)]
            elif c == 3:
                src = wo_h.at[d]
            elif c < 8:
                src = wu_h.at[d, :, :, :, pl.ds(512 * (c - 4), 512)]
            else:
                src = wd_h.at[d, pl.ds(2 * (c - 8), 2)]
            pltpu.make_async_copy(src, wts.at[d, pl.ds(2 * c, 2)], load_sem.at[d, c]).start()

    xin[0] = tok[...].astype(F32)
    row, col = iota((256, 1), 0), iota((1, 256), 1)
    q_step = ((row * 10923) >> 16).astype(F32)
    k_step = ((col * 10923) >> 16).astype(F32)
    for s in range(2):
        inv = 1.0 / lens[section, s].astype(F32)
        q_seq = jnp.floor((q_step + 0.5) * inv)
        k_seq = jnp.floor((k_step + 0.5) * inv)
        bias[s] = jnp.where((k_step <= q_step) & (q_seq == k_seq), 0.0, -1e30)
    def loaded(d, first, count):
        for c in range(first, first + count):
            at = wts.at[d, pl.ds(2 * c, 2)]
            pltpu.make_async_copy(at, at, load_sem.at[d, c]).wait()

    def forward(d, _):
        loaded(d, W_QKV, 3)
        hat, _ = ln_parts(xin[d])
        normed = (hat * gains[d, 0:1] + shifts[d, 0:1]).astype(BF)
        put_panel(acts, d, ACT_NORMED, normed)
        for c in range(3):
            put_panel(acts, d, ACT_Q + c, dot(normed, panel(wts, d, W_QKV + c)))
        for s in range(2):
            for quad in range(2):
                q = stacked(quarter(acts, d, ACT_Q, s, quad), HEAD_DIM**-0.5)
                k = quarter(acts, d, ACT_Q + 1, s, quad)
                v = quarter(acts, d, ACT_Q + 2, s, quad)
                scores = dot_lanes(q, k).reshape(4, 256, 256) + bias[s][None]
                top = jnp.max(scores, axis=-1, keepdims=True)
                e = jnp.exp(scores - top)
                total = jnp.sum(e, axis=-1, keepdims=True)
                p = (e * (1.0 / total)).astype(BF)
                for h in range(4):
                    put_quarter(acts, d, ACT_PROBS + s * 2 + quad, h // 2, h % 2, p[h])
                out = unstacked(dot(p.reshape(1024, 256), v))
                put_quarter(acts, d, ACT_ATT, s, quad, out)
        loaded(d, W_OUT, 1)
        middle = xin[d] + dot(panel(acts, d, ACT_ATT), panel(wts, d, W_OUT))
        mid[d] = middle
        loaded(d, W_UP, 4)
        hat, _ = ln_parts(middle)
        put_panel(acts, d, ACT_NORMED2, hat * gains[d, 1:2] + shifts[d, 1:2])

        def chunk(c, _):
            value, grad = gelu_pair(dot(panel(acts, d, ACT_NORMED2), panel(wts, d, W_UP + c)))
            put_panel(acts, d, ACT_GATED + c, value)
            put_panel(acts, d, ACT_SLOPE + c, grad)
            return 0

        lax.fori_loop(0, 4, chunk, 0)
        loaded(d, W_DOWN, 4)
        down = wts[d, pl.ds(2 * W_DOWN, 8)].reshape(4 * WIDTH, WIDTH)
        xin[d + 1] = mid[d] + dot(side_by_side(acts, d, ACT_GATED, 4), down)
        return 0

    lax.fori_loop(0, 2, forward, 0)
    act_mine[...] = xin[2].astype(BF)
    cot_copy.wait()
    act_copy.start()
    up = xin.at[2]
    for s in range(2):
        up[pl.ds(s * 256, 252), :] = cot[s].astype(F32)
        up[pl.ds(s * 256 + 252, 4), :] = jnp.zeros((4, WIDTH), F32)
    lng[...] = jnp.zeros_like(lng)

    def sems(k):
        return pair_sem.at[k], send_sem.at[k], recv_sem.at[k]

    def hop_rows(step):
        return pl.ds(0, 32 if step else 16)

    def piece1(k, first, hop_at):
        return Piece(
            lambda c: acts.at[2, pl.ds(c * 12 + first, 4)],
            acts.at[2, pl.ds(24 + first, 4)],
            lambda way, step: hop1.at[hop_at + step, pl.ds(4 * way, 4), hop_rows(step), :],
            mine1.at[pl.ds(first, 4)], sems(k),
        )

    def piece0(k, first, hop_at):
        return Piece(
            lambda c: acts.at[1, pl.ds(c * 12 + first, 4)],
            acts.at[1, pl.ds(24 + first, 4)],
            lambda way, step: wts.at[1, hop_at + step, pl.ds(4 * way, 4), hop_rows(step), :],
            mine0.at[pl.ds(first, 4)], sems(k),
        )

    def crossing(mine, theirs, first, k):
        return mine.at[pl.ds(first, 4)], theirs.at[pl.ds(first, 4)], cross_sem.at[k]

    down1 = Stream([piece1(0, W_DOWN, 0)], [crossing(mine1, theirs1, W_DOWN, 2)])
    up1 = Stream([piece1(1, W_UP, HOPS)], [crossing(mine1, theirs1, W_UP, 3)])
    att1 = Stream([piece1(2, 0, 2 * HOPS)], [crossing(mine1, theirs1, 0, 4)])
    down0 = Stream([piece0(3, W_DOWN, 0)], [crossing(mine0, theirs0, W_DOWN, 5)])
    up0 = Stream([piece0(4, W_UP, HOPS)], [crossing(mine0, theirs0, W_UP, 6)])
    norms = Piece(
        lambda c: lnown.at[c], lnpair, lambda way, step: lnhop.at[way, step, :, hop_rows(step), :], lnmine, sems(5)
    )
    att0 = Stream(
        [piece0(6, 0, 2 * HOPS), norms],
        [crossing(mine0, theirs0, 0, 7), (lnmine, lntheirs, cross_sem.at[8])],
    )
    encoder = Stream(
        [
            Piece(
                lambda c: genc.at[c], wts.at[1, pl.ds(21, 3)],
                lambda way, step: wts.at[1, 3 * HOPS + step, pl.ds(4 * way, 3), hop_rows(step), :],
                enc_mine, sems(7),
            ),
            Piece(
                lambda c: miscown.at[c], miscpair, lambda way, step: mischop.at[way, step, :, hop_rows(step), :],
                miscmine, sems(8),
            ),
        ],
        [],
    )
    traffic = Traffic(PLAN)

    def split(value):
        return value.astype(BF).reshape(8, 2, 32, WIDTH)

    layer_streams = {1: (down1, up1, att1), 0: (down0, up0, att0)}
    plan = {}
    for d in (1, 0):
        for n in range(8):
            plan[d, n] = traffic.take()
        traffic.add(layer_streams[d][0])
        traffic.add(layer_streams[d][1])
        for n in range(8, 13):
            plan[d, n] = traffic.take()
        if d == 1:
            traffic.add(att1)
            plan[d, 13] = traffic.take()

    def backward(i, _):
        d = 1 - i

        def each(act):
            for which in (1, 0):
                pl.when(d == which)(functools.partial(act, layer_streams[which]))

        def tick(n):
            for which in (1, 0):
                if plan[which, n]:
                    pl.when(d == which)(functools.partial(issue, plan[which, n]))

        def put(p, value):
            shaped = split(value)
            for c in range(2):
                acts[d + 1, c * 12 + p] = shaped[:, c]

        down = up[...].astype(BF)
        for c in range(4):
            part = dot_rows(panel(acts, d, ACT_GATED + c), down).astype(BF).reshape(4, 4, 32, WIDTH)
            for e in range(4):
                for j in range(4):
                    acts[d + 1, (e % 2) * 12 + W_DOWN + j, 2 * c + e // 2] = part[e, j]
            tick(c)

        @pl.when(d == 0)
        def _():
            pl.semaphore_wait(free_sem, 3)

        each(lambda streams: streams[0].pair())
        for c in range(4):
            back = dot_lanes(down, panel(wts, d, W_DOWN + c))
            back = (back * panel(acts, d, ACT_SLOPE + c).astype(F32)).astype(BF)
            put_panel(acts, d, ACT_SLOPE + c, back)
            put(W_UP + c, dot_rows(panel(acts, d, ACT_NORMED2), back))
            tick(4 + c)
        each(lambda streams: streams[1].pair())
        each(lambda streams: streams[0].open())
        back = dot_lanes(side_by_side(acts, d, ACT_SLOPE, 4), side_by_side(wts, d, W_UP, 4))
        back, gain, shift = ln_back(mid[d], back, gains[d, 1:2])
        lng[pl.ds(d * 4 + 1, 1), :] = gain
        lng[pl.ds(d * 4 + 3, 1), :] = shift
        up[...] += back
        branch = up[...].astype(BF)
        put(W_OUT, dot_rows(panel(acts, d, ACT_ATT), branch))
        back_att[...] = dot_lanes(branch, panel(wts, d, W_OUT)).astype(BF)
        each(lambda streams: streams[1].open())
        for s in range(2):
            for quad in range(2):
                rows, lanes = pl.ds(s * 256, 256), pl.ds(quad * 256, 256)
                qs = stacked(quarter(acts, d, ACT_Q, s, quad), HEAD_DIM**-0.5)
                k = quarter(acts, d, ACT_Q + 1, s, quad)
                v = quarter(acts, d, ACT_Q + 2, s, quad)
                outs = stacked(back_att[rows, lanes], 1.0)
                at = ACT_PROBS + s * 2 + quad
                p = jnp.concatenate([quarter(acts, d, at, h // 2, h % 2) for h in range(4)], axis=0)
                dp = dot_lanes(outs, v)
                pf = p.astype(F32)
                weighted = pf * dp
                total = jnp.sum(weighted, axis=-1, keepdims=True)
                ds = (weighted - pf * total).astype(BF)
                put_quarter(acts, d, ACT_Q, s, quad, unstacked(dot(ds, k)) * HEAD_DIM**-0.5)
                put_quarter(acts, d, ACT_Q + 1, s, quad, dot_rows(ds, qs))
                put_quarter(acts, d, ACT_Q + 2, s, quad, dot_rows(p, outs))
                tick(8 + 2 * s + quad)
        for c in range(3):
            put(c, dot_rows(panel(acts, d, ACT_NORMED), panel(acts, d, ACT_Q + c)))
        each(lambda streams: streams[2].pieces[0].pair_copy().start())
        tick(12)
        back = dot_lanes(side_by_side(acts, d, ACT_Q, 3), side_by_side(wts, d, W_QKV, 3))
        back, gain, shift = ln_back(xin[d], back, gains[d, 0:1])
        lng[pl.ds(d * 4, 1), :] = gain
        lng[pl.ds(d * 4 + 2, 1), :] = shift
        up[...] += back

        @pl.when(d == 1)
        def _():
            for target in (sibling, ahead, behind):
                pl.semaphore_signal(
                    free_sem, inc=1, device_id=(section, target), device_id_type=MESH
                )
            att1.open()
            issue(plan[1, 13])

        return 0

    lax.fori_loop(0, 2, backward, 0)
    eg[...] = up[...].astype(BF)
    turned = jnp.transpose(lng[...]).astype(BF).reshape(8, 2, 32, 128)
    for c in range(2):
        lnown[c, 0] = turned[:, c]
    norms.pair_copy().start()

    def fetch(k):
        i, half = k // 2, k % 2
        base = 16 * half
        copies = []
        for n, (src, lanes) in enumerate(((xl_h, 256), (bl_h, 512), (z1_h, 512), (z2_h, 512))):
            copies.append(
                pltpu.make_async_copy(
                    src.at[i, pl.ds(4 * half, 4)],
                    acts.at[0, pl.ds(base + 4 * n, 4), pl.ds(0, 7), :, pl.ds(0, lanes)],
                    stream_sem.at[half, n],
                )
            )
        return copies

    for copy in fetch(0):
        copy.start()
    att0.open()
    traffic.add(att0)
    hot = jnp.where(iota((512, TABLE), 1) == ids[...], 1.0, 0.0).astype(BF)
    code = dot_rows(eg[...], hot)
    for c in range(2):
        for half in range(2):
            genc[c, 1 + half] = split(code[:, 512 * half : 512 * (half + 1)])[:, c]
        miscown[c, 0] = code[:, CODES:].astype(BF).reshape(8, 2, 32, 128)[:, c]
    dpool[...] = dot_rows(hot[:, POOL_AT : POOL_AT + 96], eg[...])
    issue(traffic.take())
    rows = 4 * BLOCK_ROWS

    def held(ref, d, at, lanes=512):
        return ref[d, pl.ds(at, 4), pl.ds(0, 7), :, pl.ds(0, lanes)].reshape(rows, lanes)

    enc_plan = [(k, half, traffic.take()) for k in range(6) for half in range(2)]
    acc2[...] = jnp.zeros_like(acc2)
    acc1[...] = jnp.zeros_like(acc1)

    def block(k, _):
        base = 16 * (k % 2)

        def tick(half):
            for at, when, hops in enc_plan:
                if hops and when == half:
                    pl.when(k == at)(functools.partial(issue, hops))

        for copy in fetch(k):
            copy.wait()

        @pl.when(k < 5)
        def _():
            for copy in fetch(k + 1):
                copy.start()

        pooled = dpool[pl.ds(pl.multiple_of((k // 2) * 32, 32), FRAMES_BLOCK), :] * (1.0 / 64.0)
        wide = jnp.broadcast_to(pooled[:, None, :], (FRAMES_BLOCK, 8, WIDTH))
        wide = wide.reshape(BLOCK_ROWS, WIDTH)

        def part(bx, _):
            value = acts[0, base + 12 + bx, pl.ds(0, 7)].reshape(BLOCK_ROWS, WIDTH)
            back = (wide * gelu_slope(value)).astype(BF)
            wts[0, bx, pl.ds(0, 7)] = back.reshape(7, 32, WIDTH)
            value = acts[0, base + 8 + bx, pl.ds(0, 7)].reshape(BLOCK_ROWS, WIDTH)
            back = (dot_lanes(back, w2[...]) * gelu_slope(value)).astype(BF)
            wts[0, 4 + bx, pl.ds(0, 7)] = back.reshape(7, 32, WIDTH)
            return 0

        lax.fori_loop(0, 4, part, 0)
        tick(0)
        second = dot_rows(held(wts, 0, 0), held(acts, 0, base + 4))
        back = held(wts, 0, 4)
        patch = held(acts, 0, base, 256)
        first = [
            dot_rows(patch[:, 128 * dy2 : 128 * (dy2 + 1)], back[:, 256 * dy2 : 256 * (dy2 + 1)])
            for dy2 in range(2)
        ]
        first = first[0] + first[1]
        acc2[...] += second
        acc1[...] += first
        tick(1)
        return 0

    lax.fori_loop(0, 6, block, 0)
    shaped = split(acc2[...])
    hot, rest = patch_index(128)
    first = jnp.where(rest[:, :1] < 12, acc1[:, pl.ds(0, 128)], acc1[:, pl.ds(128, 128)])
    first = lax.dot_general(
        first, hot, (((0,), (0,)), ((), ())), preferred_element_type=F32,
        precision=lax.Precision.HIGHEST,
    )
    first = first.reshape(8, 2, 8, 48)
    first = jnp.concatenate([first, jnp.zeros((8, 2, 24, 48), F32)], axis=2).astype(BF)
    for c in range(2):
        genc[c, 0] = shaped[:, c]
        miscown[c, 0, :, :, pl.ds(64, 48)] = first[:, c]
    encoder.pair()
    issue(traffic.take())
    encoder.open()
    traffic.add(encoder)
    issue(traffic.take(99))
    for stream in (down1, up1, att1, down0, up0, att0):
        for crossed in stream.crossings:
            cross_copy(*crossed).wait()
    act_copy.wait()
    act[...] = act_theirs[...]
    late[...] = theirs1[...]
    early[...] = theirs0[...]
    norm[...] = lntheirs[0]
    enc[...] = enc_mine[...]
    misc[...] = miscmine[0]


def train(tok, cot, lens, gains, shifts, wq, wo, wu, wd, xl, bl, g1, g2, w2, ids):
    vm = pl.BlockSpec(memory_space=pltpu.VMEM)
    sm = pl.BlockSpec(memory_space=pltpu.SMEM)
    hb = pl.BlockSpec(memory_space=pl.ANY)

    def panels(w):
        return w.reshape(2, w.shape[1] // 256, 8, 32, w.shape[2])

    def parts(saved):
        return saved.reshape(saved.shape[0], 8, 7, 32, saved.shape[2])

    half = (8, 32, WIDTH)
    pieces = 9
    return pl.pallas_call(
        train_kernel,
        in_specs=[vm, hb, sm, vm, vm] + [hb] * 8 + [vm, vm],
        out_specs=[vm] * 7,
        out_shape=[
            jax.ShapeDtypeStruct((512, WIDTH), BF),
            jax.ShapeDtypeStruct((512, WIDTH), BF),
            jax.ShapeDtypeStruct((12, 32, WIDTH), BF),
            jax.ShapeDtypeStruct((12, 32, WIDTH), BF),
            jax.ShapeDtypeStruct((32, 128), BF),
            jax.ShapeDtypeStruct((3, 32, WIDTH), BF),
            jax.ShapeDtypeStruct((32, 128), BF),
        ],
        scratch_shapes=[
            pltpu.VMEM((2, 2 * W_PANELS) + half, BF),
            pltpu.VMEM((3, 2 * ACT_PANELS) + half, BF),
            pltpu.VMEM((3 * HOPS,) + half, BF),
            pltpu.VMEM((3, 512, WIDTH), F32),
            pltpu.VMEM((2, 512, WIDTH), F32),
            pltpu.VMEM((2, 256, 256), F32),
            pltpu.VMEM((512, WIDTH), BF),
            pltpu.VMEM((128, WIDTH), F32),
            pltpu.VMEM(cot.shape, BF),
            pltpu.VMEM((512, WIDTH), BF),
            pltpu.VMEM((512, WIDTH), BF),
            pltpu.VMEM((12, 32, WIDTH), BF),
            pltpu.VMEM((12, 32, WIDTH), BF),
            pltpu.VMEM((12, 32, WIDTH), BF),
            pltpu.VMEM((12, 32, WIDTH), BF),
            pltpu.VMEM((2, 1, 8, 32, 128), BF),
            pltpu.VMEM((1, 8, 32, 128), BF),
            pltpu.VMEM((2, HOPS, 1, 32, 128), BF),
            pltpu.VMEM((1, 32, 128), BF),
            pltpu.VMEM((1, 32, 128), BF),
            pltpu.VMEM((2, 3) + half, BF),
            pltpu.VMEM((3, 32, WIDTH), BF),
            pltpu.VMEM((2, 1, 8, 32, 128), BF),
            pltpu.VMEM((1, 8, 32, 128), BF),
            pltpu.VMEM((2, HOPS, 1, 32, 128), BF),
            pltpu.VMEM((1, 32, 128), BF),
            pltpu.VMEM((512, WIDTH), F32),
            pltpu.VMEM((128, 256), F32),
            pltpu.VMEM((96, WIDTH), F32),
            pltpu.SemaphoreType.DMA((2, W_PANELS)),
            pltpu.SemaphoreType.DMA((2, 4)),
            pltpu.SemaphoreType.DMA((9, 2)),
            pltpu.SemaphoreType.DMA((pieces, 2)),
            pltpu.SemaphoreType.DMA((pieces, 2, HOPS)),
            pltpu.SemaphoreType.DMA((pieces, 2, HOPS)),
            pltpu.SemaphoreType.REGULAR,
        ],
        compiler_params=pltpu.CompilerParams(
            collective_id=2, has_side_effects=True, vmem_limit_bytes=TRAIN_VMEM
        ),
        name="train",
    )(
        tok, cot, lens, gains, shifts, panels(wq), panels(wo), panels(wu), panels(wd),
        parts(xl), parts(bl), parts(g1), parts(g2), w2, ids,
    )


def outputs_kernel(act_in, eg_in, late, early, norm, enc, misc, *outs):
    act, eg, qkv, out, up, down, gain, bias, bias2, enc1, enc2, book, names = outs
    for s in range(2):
        act[0, s] = act_in[pl.ds(s * 256, 256), :].astype(F32)[:252].astype(BF)
        eg[0, s] = eg_in[pl.ds(s * 256, 256), :].astype(F32)[:252].astype(BF)
    for d, rows in enumerate((early, late)):
        for c in range(3):
            qkv[0, d, :, pl.ds(512 * c, 512)] = rows[W_QKV + c].astype(F32)
        out[0, d] = rows[W_OUT].astype(F32)
        for c in range(4):
            up[0, d, :, pl.ds(512 * c, 512)] = rows[W_UP + c].astype(F32)
            down[0, d, pl.ds(32 * c, 32), :] = rows[W_DOWN + c].astype(F32)
    turned = turn(norm[...].astype(F32))
    for d in range(2):
        gain[0, d] = turned[4 * d : 4 * d + 2]
        bias[0, pl.ds(d, 1)] = turned[4 * d + 2 : 4 * d + 3]
        bias2[0, pl.ds(d, 1)] = turned[4 * d + 3 : 4 * d + 4]
    enc2[0] = enc[0].astype(F32)
    for c in range(2):
        book[0, :, pl.ds(512 * c, 512)] = enc[1 + c].astype(F32)
    enc1[0] = misc[...].astype(F32)[:8, 64:112]
    turned = turn(misc[...].astype(F32))
    for a in range(17):
        names[a] = turned[a : a + 1]


def spread_outputs(*parts):
    vm = pl.BlockSpec(memory_space=pltpu.VMEM)
    shapes = [
        (1, 2, 32, 1536), (1, 2, 32, 512), (1, 2, 32, 2048), (1, 2, 128, 512), (1, 2, 2, 32),
        (1, 2, 32), (1, 2, 32), (1, 8, 48), (1, 32, 512), (1, 32, 1024), (17, 1, 32),
    ]
    acts = [jax.ShapeDtypeStruct((1, 2, 252, WIDTH), BF)] * 2
    outs = pl.pallas_call(
        outputs_kernel,
        in_specs=[vm] * len(parts),
        out_specs=[vm] * (len(shapes) + 2),
        out_shape=acts + [jax.ShapeDtypeStruct(shape, F32) for shape in shapes],
        compiler_params=pltpu.CompilerParams(vmem_limit_bytes=VMEM_LIMIT),
        name="outputs",
    )(*parts)
    outs = list(outs)
    outs[6] = outs[6].transpose(0, 1, 3, 2)
    for k in (9, 10, 11):
        outs[k] = outs[k].transpose(0, 2, 1)
    outs[12] = outs[12].transpose(1, 0, 2)
    return tuple(outs)


def swap(array):
    return lax.ppermute(array, "section", [(0, 1), (1, 0)])


def whole_rows(g):
    return g.transpose(1, 0, 2, 3).reshape(512, g.shape[-1])


def scatter_plain(g, gl, e):
    def sums(array, axis):
        return lax.psum_scatter(array.astype(F32)[None], "dp", scatter_dimension=axis, tiled=True)

    layers = [whole_rows(g[d]) for d in range(g.shape[0])]
    qkv = jnp.stack([rows[:, :1536] for rows in layers])
    out = jnp.stack([rows[:, 1536:2048] for rows in layers])
    up = jnp.stack([rows[:, 2048:4096] for rows in layers])
    down = jnp.stack(
        [
            rows[:, 4096:].reshape(16, 32, 4, WIDTH).transpose(0, 2, 1, 3).reshape(2048, WIDTH)
            for rows in layers
        ]
    )
    norm = whole_rows(gl)[:, :8].reshape(512, 2, 4).transpose(1, 0, 2)
    enc = whole_rows(e)
    first = e.transpose(1, 0, 2, 3)[:, :, :8, 1600:1648].reshape(128, 48)
    layer_sums = [sums(x, 2) for x in (qkv, out, up, down, norm)]
    layer_sums = [swap(x) for x in layer_sums]
    norm = layer_sums.pop()
    return tuple(layer_sums) + (
        norm[..., 0:2],
        norm[..., 2],
        norm[..., 3],
        sums(first.T, 2),
        sums(enc[:, :512].T, 2),
        sums(enc[:, 512:1536].T, 2),
        sums(enc[:, 1536:1553].T, 2),
    )


def on_device(
    frames, action_ids, delta_ids, seq_len, enc_w1, enc_w2, codebook, action_table,
    ln_gain, ln_bias, w_qkv, w_out, w_up, w_down, cotangent,
):
    micro, steps = frames.shape[1], frames.shape[2]
    count = micro * steps
    gains, shifts = ln_gain.transpose(0, 2, 1), ln_bias.transpose(0, 2, 1)
    tok, ids, xl, blocks, z1, z2 = enc_forward(
        frames.reshape((count,) + frames.shape[3:]), enc_w1, enc_w2, codebook, action_table,
        action_ids[0], delta_ids[0].transpose(0, 2, 1),
    )
    if lax.axis_size("dp") == 2 * CHIPS:
        parts = train(
            tok, cotangent[0], seq_len, gains, shifts, w_qkv, w_out, w_up, w_down,
            xl, blocks, z1, z2, enc_w2, ids,
        )
        return spread_outputs(*parts)
    lnp = jnp.concatenate([gains, shifts], axis=1)
    act, eg, g, gl = run_layers(tok, cotangent[0], seq_len, lnp, w_qkv, w_out, w_up, w_down)
    embed_grad = eg.reshape(micro, 256, WIDTH)[None, :, : steps * TPS]
    e = enc_backward(eg, xl, blocks, z1, z2, enc_w2, ids)
    return (act[None], embed_grad) + scatter_plain(g, gl, e)


def solution(mesh):
    return jax.shard_map(
        on_device,
        mesh=mesh,
        in_specs=(
            P("section", "dp", None, None, None),
            P("section", "dp", None),
            P("section", "dp", None, None),
            P(None, "dp"),
            P(), P(), P(), P(), P(), P(), P(), P(), P(), P(),
            P("section", "dp", None, None),
        ),
        out_specs=(
            P("section", "dp", None, None),
            P("section", "dp", None, None),
            P("section", None, "dp", None),
            P("section", None, "dp", None),
            P("section", None, "dp", None),
            P("section", None, "dp", None),
            P("section", None, "dp", None),
            P("section", None, "dp"),
            P("section", None, "dp"),
            P("section", None, "dp"),
            P("section", None, "dp"),
            P("section", None, "dp"),
            P("section", None, "dp"),
        ),
        check_vma=False,
    )
```

profile of v0, /device:TPU:0, one launch (start us, length us, event | category | flops | bytes accessed | tf_op | source)
XLA Modules:
  0.0 137.0 jit_solution(1922233312566451957)
XLA Ops:
  0.6 1.9 %copy.32 = bf16[1,2,252,512]{3,2,1,0:T(8,128)(2,1)} copy(bf16[1,2,252,512]{3,1,2,0:T(2,128)(2,1)} %param.29) | data formatting | bytes 1032192 | tf_op args[14]
  2.5 20.2 %enc_fwd.1 = (bf16[512,512]{1,0:T(8,128)(2,1)}, s32[512,1]{1,0:T(8,128)}, bf16[3,1792,256]{2,1,0:T(8,128)(2,1)}, bf16[3,1792,512]{2,1,0:T(8,128)(2,1)}, bf16[3,1...) custom-call(bf16[84,64,192]{2,1,0:T(8,128)(2,1)} %bitcast.29, bf16[48,128]{1,0:T(8,128)(2,1)} %w1.1, ...), custom_call_target="tpu_custom_call" | custom-call | tf_op jit(solution)/shard_map/enc_fwd/pallas_call | solution.py:173
  22.8 106.4 %train.1 = (bf16[512,512]{1,0:T(8,128)(2,1)}, bf16[512,512]{1,0:T(8,128)(2,1)}, bf16[12,32,512]{2,1,0:T(8,128)(2,1)}, bf16[12,32,512]{2,1,0:T(8,128)(2,1)}, bf16...) custom-call(bf16[512,512]{1,0:T(8,128)(2,1)} %get-tuple-element.39.tok, ...), custom_call_target="tpu_custom_call" | custom-call | tf_op jit(solution)/shard_map/train/pallas_call | solution.py:1096
  129.1 3.1 %outputs.1 = (bf16[1,2,252,512]{3,2,1,0:T(8,128)(2,1)}, bf16[1,2,252,512]{3,2,1,0:T(8,128)(2,1)}, f32[1,2,32,1536]{3,2,1,0:T(8,128)}, f32[1,2,32,512]{3,2,1,0:T(...) custom-call(bf16[512,512]{1,0:T(8,128)(2,1)} %get-tuple-element.45.a, ...), custom_call_target="tpu_custom_call" | custom-call | tf_op jit(solution)/shard_map/outputs/pallas_call | solution.py:1190
  132.2 2.4 %copy.29 = bf16[1,2,252,512]{3,1,2,0:T(2,128)(2,1)} copy(bf16[1,2,252,512]{3,2,1,0:T(8,128)(2,1)} %get-tuple-element.65) | data formatting | bytes 1032192
  134.6 2.4 %copy.30 = bf16[1,2,252,512]{3,1,2,0:T(2,128)(2,1)} copy(bf16[1,2,252,512]{3,2,1,0:T(8,128)(2,1)} %get-tuple-element.66) | data formatting | bytes 1032192
where the time goes:
time: 137 us
  Pallas kernels  130 us (95%)
  local copies, waits for them, and re-layouts  6.6 us (5%)
    pallas_call x1, Pallas kernels, train(): pl.pallas_call(train_kernel, in_specs=[vm, hb, sm, vm, vm] + [hb] * 8 + [...  106 us
    pallas_call x1, Pallas kernels, enc_forward(): pl.pallas_call(enc_fwd_kernel, grid=(grid,), in_specs=[pl.BlockSpec((FRAM...  20.2 us
    unnamed x3, local copies, waits for them, and re-layouts  6.6 us
    pallas_call x1, Pallas kernels, spread_outputs(): pl.pallas_call(outputs_kernel, in_specs=[vm] * len(parts), out_specs=[vm]...  3.1 us

commit v1 on v0

--- a/solution.py
+++ b/solution.py
@@ -99,9 +99,24 @@
 
 def enc_fwd_kernel(
     frames, w1, w2, book, acts, names, deltas,
-    tok, ids, xl, blocks, z1, z2, perm, lanes, big, xs, acc, table,
+    tok, ids, xl_h, bl_h, z1_h, z2_h,
+    perm, lanes, big, xs, acc, table, xl, blocks, z1, z2, sem, book_sem,
 ):
     step = pl.program_id(0)
+    book_copy = pltpu.make_async_copy(book, table.at[pl.ds(0, CODES)], book_sem)
+
+    def part_rows(bx):
+        return pl.ds(pl.multiple_of(bx * BLOCK_ROWS, BLOCK_ROWS), BLOCK_ROWS)
+
+    def save(at, bx):
+        rows = part_rows(bx)
+        return [
+            pltpu.make_async_copy(held.at[at, rows], out.at[at, rows], sem.at[at, bx, n])
+            for n, (held, out) in enumerate(((blocks, bl_h), (z1, z1_h), (z2, z2_h)))
+        ]
+
+    def save_patches(at):
+        return pltpu.make_async_copy(xl.at[at], xl_h.at[at], sem.at[at, 0, 3])
 
     @pl.when(step == 0)
     def _():
@@ -115,7 +130,7 @@
             lanes[pl.ds(256 * dy, 256), :] = jnp.where(out == dy * 24, 1.0, 0.0).astype(BF)
         xs[...] = jnp.zeros_like(xs)
         big[...] = encoder_weights(w1[...])
-        table[pl.ds(0, CODES), :] = book[...]
+        book_copy.start()
         named = acts[...].astype(F32)
         pad = jnp.zeros((TABLE - ACT_AT - named.shape[0], WIDTH), F32)
         table[pl.ds(ACT_AT, TABLE - ACT_AT), :] = jnp.concatenate([named, pad], axis=0).astype(BF)
@@ -128,20 +143,23 @@
     for dy2 in range(2):
         spread = dot(xs[dy2], lanes[...]).astype(BF)
         for bx in range(8):
-            xl[0, pl.ds(bx * BLOCK_ROWS, BLOCK_ROWS), pl.ds(dy2 * 128, 128)] = spread[
+            xl[step, pl.ds(bx * BLOCK_ROWS, BLOCK_ROWS), pl.ds(dy2 * 128, 128)] = spread[
                 :, bx * 128 : (bx + 1) * 128
             ]
+    save_patches(step).start()
     acc[...] = jnp.zeros_like(acc)
 
     def part(bx, _):
-        rows = pl.ds(pl.multiple_of(bx * BLOCK_ROWS, BLOCK_ROWS), BLOCK_ROWS)
-        first = dot(xl[0, rows, :], big[...])
-        z1[0, rows, :] = first.astype(BF)
+        rows = part_rows(bx)
+        first = dot(xl[step, rows, :], big[...])
+        z1[step, rows, :] = first.astype(BF)
         value = gelu(first).astype(BF)
-        blocks[0, rows, :] = value
+        blocks[step, rows, :] = value
         second = dot(value, w2[...])
-        z2[0, rows, :] = second.astype(BF)
+        z2[step, rows, :] = second.astype(BF)
         acc[...] += gelu(second)
+        for copy in save(step, bx):
+            copy.start()
         return 0
 
     lax.fori_loop(0, 8, part, 0, unroll=True)
@@ -151,12 +169,18 @@
 
     @pl.when(step == pl.num_programs(0) - 1)
     def _():
+        book_copy.wait()
         for s in range(2):
             rows = pl.ds(s * 256, 256)
             found = token_ids(s, names[...], deltas[...])
             ids[rows, :] = found
             hot = jnp.where(iota((256, TABLE), 1) == found, 1.0, 0.0).astype(BF)
             tok[rows, :] = dot(hot, table[...]).astype(BF)
+        for at in range(xl.shape[0]):
+            save_patches(at).wait()
+            for bx in range(8):
+                for copy in save(at, bx):
+                    copy.wait()
 
 
 def enc_forward(frames, w1, w2, book, acts, names, deltas):
@@ -167,9 +191,7 @@
     def whole(shape):
         return pl.BlockSpec(shape, lambda i: (0,) * len(shape))
 
-    def saved(lanes):
-        return pl.BlockSpec((1, rows, lanes), lambda i: (i, 0, 0))
-
+    hb = pl.BlockSpec(memory_space=pl.ANY)
     return pl.pallas_call(
         enc_fwd_kernel,
         grid=(grid,),
@@ -177,13 +199,13 @@
             pl.BlockSpec((FRAMES_BLOCK, 64, 192), lambda i: (i, 0, 0)),
             whole(w1.shape),
             whole(w2.shape),
-            whole(book.shape),
+            hb,
             whole(acts.shape),
             whole(names.shape),
             whole(deltas.shape),
         ],
         out_specs=[
-            whole((512, WIDTH)), whole((512, 1)), saved(256), saved(512), saved(512), saved(512),
+            whole((512, WIDTH)), whole((512, 1)), hb, hb, hb, hb,
         ],
         out_shape=[
             jax.ShapeDtypeStruct((512, WIDTH), BF),
@@ -200,6 +222,12 @@
             pltpu.VMEM((2, BLOCK_ROWS, 1024), BF),
             pltpu.VMEM((BLOCK_ROWS, WIDTH), F32),
             pltpu.VMEM((TABLE, WIDTH), BF),
+            pltpu.VMEM((grid, rows, 256), BF),
+            pltpu.VMEM((grid, rows, 512), BF),
+            pltpu.VMEM((grid, rows, 512), BF),
+            pltpu.VMEM((grid, rows, 512), BF),
+            pltpu.SemaphoreType.DMA((grid, 8, 4)),
+            pltpu.SemaphoreType.DMA,
         ],
         compiler_params=pltpu.CompilerParams(vmem_limit_bytes=VMEM_LIMIT),
         name="enc_fwd",
@@ -793,7 +821,7 @@
             put_panel(acts, d, ACT_SLOPE + c, grad)
             return 0
 
-        lax.fori_loop(0, 4, chunk, 0)
+        lax.fori_loop(0, 4, chunk, 0, unroll=True)
         loaded(d, W_DOWN, 4)
         down = wts[d, pl.ds(2 * W_DOWN, 8)].reshape(4 * WIDTH, WIDTH)
         xin[d + 1] = mid[d] + dot(side_by_side(acts, d, ACT_GATED, 4), down)
@@ -804,8 +832,9 @@
     cot_copy.wait()
     act_copy.start()
     up = xin.at[2]
+    wide = cot[...].astype(F32)
     for s in range(2):
-        up[pl.ds(s * 256, 252), :] = cot[s].astype(F32)
+        up[pl.ds(s * 256, 252), :] = wide[:, s]
         up[pl.ds(s * 256 + 252, 4), :] = jnp.zeros((4, WIDTH), F32)
     lng[...] = jnp.zeros_like(lng)
 
@@ -1156,9 +1185,9 @@
 
 def outputs_kernel(act_in, eg_in, late, early, norm, enc, misc, *outs):
     act, eg, qkv, out, up, down, gain, bias, bias2, enc1, enc2, book, names = outs
-    for s in range(2):
-        act[0, s] = act_in[pl.ds(s * 256, 256), :].astype(F32)[:252].astype(BF)
-        eg[0, s] = eg_in[pl.ds(s * 256, 256), :].astype(F32)[:252].astype(BF)
+    for source, target in ((act_in, act), (eg_in, eg)):
+        slots = [source[pl.ds(s * 256, 256), :].astype(F32)[:252] for s in range(2)]
+        target[0] = jnp.stack(slots, axis=1).astype(BF)
     for d, rows in enumerate((early, late)):
         for c in range(3):
             qkv[0, d, :, pl.ds(512 * c, 512)] = rows[W_QKV + c].astype(F32)
@@ -1186,7 +1215,7 @@
         (1, 2, 32, 1536), (1, 2, 32, 512), (1, 2, 32, 2048), (1, 2, 128, 512), (1, 2, 2, 32),
         (1, 2, 32), (1, 2, 32), (1, 8, 48), (1, 32, 512), (1, 32, 1024), (17, 1, 32),
     ]
-    acts = [jax.ShapeDtypeStruct((1, 2, 252, WIDTH), BF)] * 2
+    acts = [jax.ShapeDtypeStruct((1, 252, 2, WIDTH), BF)] * 2
     outs = pl.pallas_call(
         outputs_kernel,
         in_specs=[vm] * len(parts),
@@ -1195,7 +1224,7 @@
         compiler_params=pltpu.CompilerParams(vmem_limit_bytes=VMEM_LIMIT),
         name="outputs",
     )(*parts)
-    outs = list(outs)
+    outs = [x.transpose(0, 2, 1, 3) for x in outs[:2]] + list(outs[2:])
     outs[6] = outs[6].transpose(0, 1, 3, 2)
     for k in (9, 10, 11):
         outs[k] = outs[k].transpose(0, 2, 1)
@@ -1255,7 +1284,7 @@
     )
     if lax.axis_size("dp") == 2 * CHIPS:
         parts = train(
-            tok, cotangent[0], seq_len, gains, shifts, w_qkv, w_out, w_up, w_down,
+            tok, cotangent[0].transpose(1, 0, 2), seq_len, gains, shifts, w_qkv, w_out, w_up, w_down,
             xl, blocks, z1, z2, enc_w2, ids,
         )
         return spread_outputs(*parts)

time: 137 us -> 130 us (0.949)
  local copies, waits for them, and re-layouts: 6.6 us -> 0 us
    unnamed x3 -> x0, local copies, waits for them, and re-layouts: 6.6 us -> none
    pallas_call x1, Pallas kernels: 3.1 us -> 4.76 us  [spread_outputs(): pl.pallas_call(outputs_kernel, in_specs=[vm] * len(parts), out_specs=[vm]...]
    pallas_call x1, Pallas kernels: 20.2 us -> 18.6 us  [enc_forward(): pl.pallas_call(enc_fwd_kernel, grid=(grid,), in_specs=[pl.BlockSpec((FRAM...]
where the time goes in v1:
time: 130 us; the launch traced here: 129 us
  Pallas kernels  129 us (99%)
    pallas_call x1, Pallas kernels, train(): pl.pallas_call(train_kernel, in_specs=[vm, hb, sm, vm, vm] + [hb] * 8 + [...  105 us
    pallas_call x1, Pallas kernels, enc_forward(): pl.pallas_call(enc_fwd_kernel, grid=(grid,), in_specs=[pl.BlockSpec((FRAM...  18.6 us
    pallas_call x1, Pallas kernels, spread_outputs(): pl.pallas_call(outputs_kernel, in_specs=[vm] * len(parts), out_specs=[vm]...  4.76 us

profile of v1, /device:TPU:0, one launch (start us, length us, event | category | flops | bytes accessed | tf_op | source)
XLA Modules:
  0.0 129.4 jit_solution(7906326377163942746)
XLA Ops:
  0.6 18.6 %enc_fwd.1 = (bf16[512,512]{1,0:T(8,128)(2,1)}, s32[512,1]{1,0:T(8,128)}, bf16[3,1792,256]{2,1,0:T(8,128)(2,1)}, bf16[3,1792,512]{2,1,0:T(8,128)(2,1)}, bf16[3,1...) custom-call(bf16[84,64,192]{2,1,0:T(8,128)(2,1)} %bitcast.31, bf16[48,128]{1,0:T(8,128)(2,1)} %w1.1, ...), custom_call_target="tpu_custom_call" | custom-call | tf_op jit(solution)/shard_map/enc_fwd/pallas_call | solution.py:195
  19.3 105.2 %train.1 = (bf16[512,512]{1,0:T(8,128)(2,1)}, bf16[512,512]{1,0:T(8,128)(2,1)}, bf16[12,32,512]{2,1,0:T(8,128)(2,1)}, bf16[12,32,512]{2,1,0:T(8,128)(2,1)}, bf16...) custom-call(bf16[512,512]{1,0:T(8,128)(2,1)} %get-tuple-element.39.tok, ...), custom_call_target="tpu_custom_call" | custom-call | tf_op jit(solution)/shard_map/train/pallas_call | solution.py:1125
  124.5 4.8 %outputs.1 = (bf16[1,252,2,512]{3,2,1,0:T(2,128)(2,1)}, bf16[1,252,2,512]{3,2,1,0:T(2,128)(2,1)}, f32[1,2,32,1536]{3,2,1,0:T(8,128)}, f32[1,2,32,512]{3,2,1,0:T(...) custom-call(bf16[512,512]{1,0:T(8,128)(2,1)} %get-tuple-element.45.a, ...), custom_call_target="tpu_custom_call" | custom-call | tf_op jit(solution)/shard_map/outputs/pallas_call | solution.py:1219

commit v2 on v1

--- a/solution.py
+++ b/solution.py
@@ -26,7 +26,7 @@
 ENC_COLS = 1664
 VMEM_LIMIT = 60 << 20
 TRAIN_VMEM = 63 << 20
-PLAN = "00000000010111000000001111110101010101012"
+PLAN = "00000000010110010000001111110101010101012"
 
 
 def dot(a, b):

time: 130 us -> 129 us (level)
  no operation moved by 1% of the time
where the time goes in v2:
time: 129 us; the launch traced here: 128 us
  Pallas kernels  128 us (99%)
    pallas_call x1, Pallas kernels, train(): pl.pallas_call(train_kernel, in_specs=[vm, hb, sm, vm, vm] + [hb] * 8 + [...  104 us
    pallas_call x1, Pallas kernels, enc_forward(): pl.pallas_call(enc_fwd_kernel, grid=(grid,), in_specs=[pl.BlockSpec((FRAM...  18.6 us
    pallas_call x1, Pallas kernels, spread_outputs(): pl.pallas_call(outputs_kernel, in_specs=[vm] * len(parts), out_specs=[vm]...  4.76 us

profile of v2, /device:TPU:0, one launch (start us, length us, event | category | flops | bytes accessed | tf_op | source)
XLA Modules:
  0.0 128.5 jit_solution(9569048097876025075)
XLA Ops:
  0.6 18.6 %enc_fwd.1 = (bf16[512,512]{1,0:T(8,128)(2,1)}, s32[512,1]{1,0:T(8,128)}, bf16[3,1792,256]{2,1,0:T(8,128)(2,1)}, bf16[3,1792,512]{2,1,0:T(8,128)(2,1)}, bf16[3,1...) custom-call(bf16[84,64,192]{2,1,0:T(8,128)(2,1)} %bitcast.31, bf16[48,128]{1,0:T(8,128)(2,1)} %w1.1, ...), custom_call_target="tpu_custom_call" | custom-call | tf_op jit(solution)/shard_map/enc_fwd/pallas_call | solution.py:195
  19.3 104.2 %train.1 = (bf16[512,512]{1,0:T(8,128)(2,1)}, bf16[512,512]{1,0:T(8,128)(2,1)}, bf16[12,32,512]{2,1,0:T(8,128)(2,1)}, bf16[12,32,512]{2,1,0:T(8,128)(2,1)}, bf16...) custom-call(bf16[512,512]{1,0:T(8,128)(2,1)} %get-tuple-element.39.tok, ...), custom_call_target="tpu_custom_call" | custom-call | tf_op jit(solution)/shard_map/train/pallas_call | solution.py:1125
  123.5 4.8 %outputs.1 = (bf16[1,252,2,512]{3,2,1,0:T(2,128)(2,1)}, bf16[1,252,2,512]{3,2,1,0:T(2,128)(2,1)}, f32[1,2,32,1536]{3,2,1,0:T(8,128)}, f32[1,2,32,512]{3,2,1,0:T(...) custom-call(bf16[512,512]{1,0:T(8,128)(2,1)} %get-tuple-element.45.a, ...), custom_call_target="tpu_custom_call" | custom-call | tf_op jit(solution)/shard_map/outputs/pallas_call | solution.py:1219
